TPU v7x, 256 devices: a whole 4x4x8 slice. The times are simulated.
256 devices in a mesh: scen: 4 (over z_lo, core), tile: 64 (over z_hi, x, y).
Axes of the slice: x: 4, y: 4, z: 8 (z_hi: 4, z_lo: 2; z = z_hi * 2 + z_lo), core: 2. Of those that a mesh axis runs over, the one named last changes fastest.
Arguments:
- initial_heads: bfloat16 [512, 256, 512], P('scen', 'tile'), may hold values from -6 to 6
- diffusivity: float32 [256, 512], P('tile'), may hold values from 0.03 to 0.24
- recharge_map: float32 [256, 512], P('tile'), may hold values from 0.2 to 2
- rate_table: float32 [8, 4], replicated, may hold values from 0 to 0.5
- recharge_ids: int32 [512], P('scen'), may hold values from 0 to 7
- monitor_cells: int32 [4096], P('tile'), may hold values from 0 to 2047, as said below
- well_cells: int32 [512], P('tile'), may hold values from 0 to 2047, as said below
- targets: float32 [4096], P('tile'), may hold values from -3 to 3
- w_in: bfloat16 [4096, 2048], P('tile'), may hold values from -0.09375 to 0.09375
- b_in: float32 [2048], P('tile'), may hold values from -3 to 3
- w_mid: bfloat16 [2048, 2048], P('tile'), may hold values from -0.125 to 0.125
- b_mid: float32 [2048], P('tile'), may hold values from -3 to 3
- w_out: bfloat16 [2048, 512], P('tile'), may hold values from -0.125 to 0.125
- b_out: float32 [512], P('tile'), may hold values from -3 to 3
Outputs:
- final_heads: bfloat16 [512, 4096], P('scen', 'tile')
- g_w_in: float32 [4096, 2048], P('tile')
- g_b_in: float32 [2048], P('tile')
- g_w_mid: float32 [2048, 2048], P('tile')
- g_b_mid: float32 [2048], P('tile')
- g_w_out: float32 [2048, 512], P('tile')
- g_b_out: float32 [512], P('tile')
Inputs may be any that keep to these rules, and one draw needn't show every extreme that they name: `monitor_cells`: each entry is a cell of its own slab, numbered row by row over its 4 x 512 cells. `well_cells`: each entry is a cell of its own slab, numbered row by row over its 4 x 512 cells.
All inputs are finite; a program needn't handle non-finite values.
Results may differ from a plain program's by a relative error of at most 0.009.
Values may be sent and summed in bfloat16 or wider, within the bound.
No kernel may reach another device: no remote copies, remote signals or barrier semaphores. Data moves between devices by JAX's collectives and lax.ppermute only.
A program may use at most 64 MiB of HBM per device.

v0:
```python
import math

import jax
import jax.numpy as jnp
from jax import lax
from jax.sharding import PartitionSpec as P


def with_halo(block, sides, width):
    for axis, dim in sides:
        count = lax.axis_size(axis)
        forward = [(i, i + 1) for i in range(count - 1)]
        backward = [(target, source) for source, target in forward]
        low = lax.ppermute(
            lax.slice_in_dim(block, block.shape[dim] - width, None, axis=dim), axis, forward
        )
        high = lax.ppermute(lax.slice_in_dim(block, 0, width, axis=dim), axis, backward)
        block = jnp.concatenate([low, block, high], axis=dim)
    return block


def laplace(padded_rows, center):
    padded = jnp.pad(padded_rows, ((0, 0), (0, 0), (1, 1)))
    return (
        padded[:, 2:, 1:-1]
        + padded[:, :-2, 1:-1]
        + padded[:, 1:-1, 2:]
        + padded[:, 1:-1, :-2]
        - 4.0 * center
    )


def column_term(weight, activ):
    return lax.dot_general(
        weight, activ, (((0,), (0,)), ((), ())), preferred_element_type=jnp.float32
    )


def back_step(weight, activ, piece):
    g_act = jnp.dot(weight, piece, preferred_element_type=jnp.float32)
    block = lax.dot_general(
        activ, piece, (((1,), (1,)), ((), ())), preferred_element_type=jnp.float32
    )
    return (g_act, block)


def per_device(
    initial_heads,
    diffusivity,
    recharge_map,
    rate_table,
    recharge_ids,
    monitor_cells,
    well_cells,
    targets,
    w_in,
    b_in,
    w_mid,
    b_mid,
    w_out,
    b_out,
):
    members, rows, cols = initial_heads.shape
    cells = rows * cols
    grand = members * lax.axis_size("scen")
    steps = rate_table.shape[1]
    positions = jnp.arange(cells, dtype=jnp.int32)
    monitor_hot = (monitor_cells[:, None] == positions[None, :]).astype(jnp.float32)
    monitor_pick = monitor_hot.astype(jnp.bfloat16)
    well_hot = (well_cells[:, None] == positions[None, :]).astype(jnp.float32)
    observed = lax.dot_general(
        initial_heads.reshape(members, cells),
        monitor_pick,
        (((1,), (1,)), ((), ())),
        preferred_element_type=jnp.float32,
    ).astype(jnp.bfloat16)
    first_pre = lax.psum_scatter(
        lax.dot_general(
            w_in, observed, (((0,), (1,)), ((), ())), preferred_element_type=jnp.float32
        ),
        "tile",
        scatter_dimension=0,
        tiled=True,
    )
    act1 = jnp.tanh(first_pre + b_in[:, None]).astype(jnp.bfloat16)
    middle_pre = lax.psum_scatter(column_term(w_mid, act1), "tile", scatter_dimension=0, tiled=True)
    act2 = jnp.tanh(middle_pre + b_mid[:, None]).astype(jnp.bfloat16)
    pre3 = (
        lax.psum_scatter(column_term(w_out, act2), "tile", scatter_dimension=0, tiled=True)
        + b_out[:, None]
    )
    rates = 0.5 * jax.nn.softplus(pre3)
    sink = lax.dot_general(
        rates, well_hot, (((0,), (0,)), ((), ())), precision=lax.Precision.HIGHEST
    ).reshape(members, rows, cols)
    codes = jnp.arange(rate_table.shape[0], dtype=jnp.int32)
    pattern_hot = (recharge_ids[:, None] == codes[None, :]).astype(jnp.float32)
    monthly = jnp.dot(pattern_hot, rate_table, precision=lax.Precision.HIGHEST)
    heads = initial_heads
    for step in range(steps):
        padded = with_halo(heads, (("tile", 1),), 1)
        current = heads.astype(jnp.float32)
        heads = (
            current
            + diffusivity * laplace(padded.astype(jnp.float32), current)
            + monthly[:, step][:, None, None] * recharge_map
            - sink
        ).astype(jnp.bfloat16)
    final_heads = lax.dot_general(
        heads.reshape(members, cells),
        monitor_pick,
        (((1,), (1,)), ((), ())),
        preferred_element_type=jnp.float32,
    ).astype(jnp.bfloat16)
    spread = (final_heads.astype(jnp.float32) - targets[None, :]) / math.sqrt(grand)
    adjoint = jnp.dot(spread, monitor_hot, precision=lax.Precision.HIGHEST).reshape(
        members, rows, cols
    )
    total = adjoint
    for step in range(steps - 1):
        weighted = diffusivity * adjoint
        padded = with_halo(weighted, (("tile", 1),), 1)
        adjoint = adjoint + laplace(padded, weighted)
        total = total + adjoint
    well_grad = -lax.dot_general(
        well_hot,
        total.reshape(members, cells),
        (((1,), (1,)), ((), ())),
        precision=lax.Precision.HIGHEST,
    )
    g3 = (well_grad * 0.5 * jax.nn.sigmoid(pre3)).astype(jnp.bfloat16)
    g_b_out = jnp.sum(g3.astype(jnp.float32), axis=1)
    g_act2, g_w_out = back_step(w_out, act2, lax.all_gather(g3, "tile", axis=0, tiled=True))
    act2_f = act2.astype(jnp.float32)
    g2 = (g_act2 * (1.0 - act2_f * act2_f)).astype(jnp.bfloat16)
    g_b_mid = jnp.sum(g2.astype(jnp.float32), axis=1)
    g_act1, g_w_mid = back_step(w_mid, act1, lax.all_gather(g2, "tile", axis=0, tiled=True))
    act1_f = act1.astype(jnp.float32)
    g1 = (g_act1 * (1.0 - act1_f * act1_f)).astype(jnp.bfloat16)
    g_b_in = jnp.sum(g1.astype(jnp.float32), axis=1)
    g_w_in = lax.dot_general(
        observed,
        lax.all_gather(g1, "tile", axis=0, tiled=True),
        (((0,), (1,)), ((), ())),
        preferred_element_type=jnp.float32,
    )
    g_w_in, g_b_in, g_w_mid, g_b_mid, g_w_out, g_b_out = lax.psum(
        (g_w_in, g_b_in, g_w_mid, g_b_mid, g_w_out, g_b_out), "scen"
    )
    return (final_heads, g_w_in, g_b_in, g_w_mid, g_b_mid, g_w_out, g_b_out)


def solution(mesh):
    return jax.shard_map(
        per_device,
        mesh=mesh,
        in_specs=(
            P("scen", "tile", None),
            P("tile", None),
            P("tile", None),
            P(),
            P("scen"),
            P("tile"),
            P("tile"),
            P("tile"),
            P("tile", None),
            P("tile"),
            P("tile", None),
            P("tile"),
            P("tile", None),
            P("tile"),
        ),
        out_specs=(
            P("scen", "tile"),
            P("tile", None),
            P("tile"),
            P("tile", None),
            P("tile"),
            P("tile", None),
            P("tile"),
        ),
        check_vma=False,
    )
```

profile of v0, /device:TPU:1, one launch (start us, length us, event | category | flops | bytes accessed | tf_op | source)
XLA Modules:
  0.0 2199.0 jit_solution(5396997181996519392)
XLA Ops:
  10.4 1.3 copy.64
  11.8 335.4 %reduce-scatter.8.cloned.1.call-done = f32[32,128]{1,0:T(8,128)} async-done(((f32[2048,128]{1,0:T(8,128)}), f32[32,128]{1,0:T(8,128)}) %reduce-scatter.8.cloned.1.call-update) | async-done | bytes 16400 | tf_op jit(solution)/shard_map/reduce_scatter | solution.py:77
  353.0 374.5 %reduce-scatter.10.cloned.1.call-done = f32[32,128]{1,0:T(8,128)} async-done(((f32[2048,128]{1,0:T(8,128)}), f32[32,128]{1,0:T(8,128)}) %reduce-scatter.10.cloned.1.call-update) | async-done | bytes 16400 | tf_op jit(solution)/shard_map/reduce_scatter | solution.py:86
  730.8 692.2 %all-reduce.13.cloned.1.call-done = f32[512,128]{0,1:T(8,128)} async-done(((f32[512,128]{0,1:T(8,128)}), f32[512,128]{0,1:T(8,128)}) %all-reduce.13.cloned.1.call-update) | async-done | bytes 262160
  1429.2 4.2 collective-permute-done.3
  1434.3 2.5 collective-permute-start.4
  1438.8 4.2 collective-permute-done.5
  1443.9 2.2 collective-permute-start.6
  1448.1 3.8 collective-permute-done.7
  1454.6 3.3 collective-permute-start.9
  1459.2 2.0 collective-permute-done.9
  1461.2 4.0 collective-permute-done.8
  1468.2 5.2 collective-permute-start.11
  1473.5 2.1 collective-permute-done.10
  1478.5 2.4 broadcast_multiply_fusion
  1482.4 5.3 collective-permute-start.13
  1488.8 1.5 collective-permute-done.13
  1494.2 169.2 %all_gather.9 = bf16[512,128]{1,0:T(8,128)(2,1)S(1)} all-gather(bf16[8,128]{1,0:T(8,128)(2,1)S(1)} %get-tuple-element.40), channel_id=1, replica_groups=mesh['scen'=4,'tile'=64] {'tile'}, dimensions={0}, use_global_device_ids=true | all-gather | bytes 133120 | tf_op jit(solution)/shard_map/all_gather | solution.py:133
  1664.5 158.8 %all_gather.10 = bf16[2048,128]{1,0:T(8,128)(2,1)S(1)} all-gather(bf16[32,128]{1,0:T(8,128)(2,1)S(1)} %get-tuple-element.38), channel_id=1, replica_groups=mesh['scen'=4,'tile'=64] {'tile'}, dimensions={0}, use_global_device_ids=true | all-gather | bytes 532480 | tf_op jit(solution)/shard_map/all_gather | solution.py:137
  1824.6 160.6 %all_gather.11 = bf16[2048,128]{1,0:T(8,128)(2,1)S(1)} all-gather(bf16[32,128]{1,0:T(8,128)(2,1)S(1)} %get-tuple-element.36), channel_id=1, replica_groups=mesh['scen'=4,'tile'=64] {'tile'}, dimensions={0}, use_global_device_ids=true | all-gather | bytes 532480 | tf_op jit(solution)/shard_map/all_gather | solution.py:143
  1986.3 122.5 %all-reduce.8 = (f32[32]{0:T(128)}, f32[32]{0:T(128)}, f32[8]{0:T(128)}) all-reduce(f32[32]{0:T(128)S(1)} %get-tuple-element.35, f32[32]{0:T(128)S(1)} %get-tuple-element.37, f32[8]{0:T(128)S(1)} %get-tuple-element.39), channel_id=1, replica_groups=mesh['scen'=4,'tile'=64] {'scen'}, use_global_device_ids=true, to_apply=%region_5.6 | all-reduce | flops 72 | bytes 576 | tf_op jit(solution)/shard_map/psum | solution.py:147
  2108.8 79.5 %all-reduce.15.cloned.1.call-done = (f32[64,2048]{1,0:T(8,128)}, f32[32,2048]{1,0:T(8,128)}, f32[32,512]{1,0:T(8,128)}) async-done(((f32[64,2048]{1,0:T(8,128)}, f32[32,2048]{1,0:T(8,128)}, f32[32,512]{1,0:T(8,128)}), (f32[64,2048]{1,0:T(8,128)}, f32[32,2048]{1,0:T(8,128)}, f32[32,512]{1,0:T(8,128)})) %all-reduce.15.cloned.1.call-update) | async-done | bytes 851984 | tf_op jit(solution)/shard_map/psum | solution.py:147
  2188.2 1.9 copy.77
  2190.1 1.7 copy.78
  (139 shorter events, 43.7 us)
Async XLA Ops:
  7.2 340.0 %reduce-scatter.8.cloned.1.call-start = ((), (), s32[]{:S(2)}) async-start(), calls=%async_computation.2 | async-start | bytes 1064960 | tf_op jit(solution)/shard_map/reduce_scatter | solution.py:77
  11.7 715.8 %reduce-scatter.10.cloned.1.call-start = ((), (), s32[]{:S(2)}) async-start(), calls=%async_computation.3 | async-start | bytes 1064960 | tf_op jit(solution)/shard_map/reduce_scatter | solution.py:86
  349.6 379.7 %copy-start.30 = (u32[256]{0:T(256)S(1)}, u32[256]{0:T(256)}, u32[]{:S(2)}) copy-start(u32[256]{0:T(256)} %constant.41) | copy-start | bytes 3076
  349.6 1073.3 %all-reduce.13.cloned.1.call-start = ((), (), s32[]{:S(2)}) async-start(), calls=%async_computation.4 | async-start | bytes 524288
  350.2 380.5 %collective-permute-start = (bf16[128,1,512]{0,2,1:T(8,128)(2,1)S(1)}, bf16[128,1,512]{0,2,1:T(8,128)(2,1)S(1)}, u32[]{:S(2)}, u32[]{:S(2)}) collective-permute-start(bf16[128,1,512]{0,2,1:T(8,128)(2,1)S(1)} %get-tuple-element.29), channel_id=1, source_target_pairs={{0,1},{1,2},{2,3},{3,4},{4,5},{5,6},{6,7},{7,8},{8,9},{9,10},{10,1... | collective-permute-start | bytes 393224 | tf_op jit(solution)/shard_map/ppermute | solution.py:14
  351.5 379.2 %collective-permute-start.1 = (bf16[128,1,512]{0,2,1:T(8,128)(2,1)S(1)}, bf16[128,1,512]{0,2,1:T(8,128)(2,1)S(1)}, u32[]{:S(2)}, u32[]{:S(2)}) collective-permute-start(bf16[128,1,512]{0,2,1:T(8,128)(2,1)S(1)} %get-tuple-element.30), channel_id=1, source_target_pairs={{1,0},{2,1},{3,2},{4,3},{5,4},{6,5},{7,6},{8,7},{9,8},{10,9},{11,1... | collective-permute-start | bytes 393224 | tf_op jit(solution)/shard_map/ppermute | solution.py:17
  353.0 1071.0 %copy-start.20 = (s32[8]{0:T(128)S(1)}, s32[8]{0:T(128)}, u32[]{:S(2)}) copy-start(s32[8]{0:T(128)} %param.20) | copy-start | bytes 100
  353.0 1071.0 %copy-start.22 = (f32[8]{0:T(128)S(1)}, f32[8]{0:T(128)}, u32[]{:S(2)}) copy-start(f32[8]{0:T(128)} %param.27) | copy-start | bytes 100
  729.3 1459.0 %all-reduce.15.cloned.1.call-start = ((), (), s32[]{:S(2)}) async-start(), calls=%async_computation.5 | async-start | bytes 1703936 | tf_op jit(solution)/shard_map/psum | solution.py:147
  730.6 694.5 %copy-start.8 = (f32[4,512]{1,0:T(4,128)S(1)}, f32[4,512]{1,0:T(4,128)}, u32[]{:S(2)}) copy-start(f32[4,512]{1,0:T(4,128)} %param.15) | copy-start | bytes 24580
  730.6 694.5 %copy-start.9 = (f32[4,512]{1,0:T(4,128)S(1)}, f32[4,512]{1,0:T(4,128)}, u32[]{:S(2)}) copy-start(f32[4,512]{1,0:T(4,128)} %param.16) | copy-start | bytes 24580
  1425.9 3.2 collective-permute-start.2
  1427.2 6.1 collective-permute-start.3
  1434.3 4.5 collective-permute-start.4
  1436.9 6.1 collective-permute-start.5
  1443.9 4.1 collective-permute-start.6
  1446.2 5.7 collective-permute-start.7
  1454.6 6.6 collective-permute-start.9
  1457.9 7.3 collective-permute-start.8
  1466.8 8.8 collective-permute-start.10
  1468.2 7.8 collective-permute-start.11
  1481.0 7.7 collective-permute-start.12
  1482.4 7.9 collective-permute-start.13
  1494.2 491.0 %copy-start.15 = (bf16[64,128]{1,0:T(8,128)(2,1)S(1)}, bf16[64,128]{1,0:T(8,128)(2,1)}, u32[]{:S(2)}) copy-start(bf16[64,128]{1,0:T(8,128)(2,1)} %copy-done.14) | copy-start | bytes 49156
  (25 other events, 1800.9 us)
Sparse Core Ops, SparseCore 0:
  11.9 335.2 reduce-scatter.7
  349.8 377.6 reduce-scatter.9
  730.7 692.2 all-reduce.12
  1986.4 201.7 all-reduce.14
where the time goes:
time: 2200 us
  waiting for transfers between devices  1510 us (69%)
  blocking collectives  611 us (28%)
  starting transfers between devices  30.4 us (1%)
    unnamed x5, waiting for transfers between devices  692 us
    reduce_scatter x1, waiting for transfers between devices, per_device(): lax.psum_scatter(column_term(w_mid, act1), 'tile', scatter_dimension=0, t...  375 us
    reduce_scatter x1, waiting for transfers between devices, per_device(): lax.psum_scatter(lax.dot_general(w_in, observed, (((0,), (1,)), ((), ()))...  335 us
    all_gather x1, blocking collectives, per_device(): lax.all_gather(g3, 'tile', axis=0, tiled=True)  169 us
    all_gather x1, blocking collectives, per_device(): lax.all_gather(g1, 'tile', axis=0, tiled=True)  161 us
    all_gather x1, blocking collectives, per_device(): lax.all_gather(g2, 'tile', axis=0, tiled=True)  159 us
    psum x1, blocking collectives, per_device(): lax.psum((g_w_in, g_b_in, g_w_mid, g_b_mid, g_w_out, g_b_out), 'scen')  122 us
    psum x1, waiting for transfers between devices, per_device(): lax.psum((g_w_in, g_b_in, g_w_mid, g_b_mid, g_w_out, g_b_out), 'scen')  79.5 us
  transfers between devices with their start and end apart: 18, of which 16 were waited for; matrix products, arithmetic and copies ran while one was open for 0% of the time, Pallas kernels for 0%

commit v1 on v0

--- a/solution.py
+++ b/solution.py
@@ -28,6 +28,20 @@
         + padded[:, 1:-1, :-2]
         - 4.0 * center
     )
+
+
+def scatter_sum(terms):
+    count = lax.axis_size("tile")
+    parts = terms.reshape((count, terms.shape[0] // count) + terms.shape[1:])
+    parts = lax.all_to_all(parts, "tile", 0, 0, tiled=True)
+    return jnp.sum(parts, axis=0)
+
+
+def gather(block):
+    count = lax.axis_size("tile")
+    copies = jnp.broadcast_to(block[None], (count,) + block.shape)
+    got = lax.all_to_all(copies, "tile", 0, 0, tiled=True)
+    return got.reshape((count * block.shape[0],) + block.shape[1:])
 
 
 def column_term(weight, activ):
@@ -74,19 +88,16 @@
         (((1,), (1,)), ((), ())),
         preferred_element_type=jnp.float32,
     ).astype(jnp.bfloat16)
-    first_pre = lax.psum_scatter(
+    first_pre = scatter_sum(
         lax.dot_general(
             w_in, observed, (((0,), (1,)), ((), ())), preferred_element_type=jnp.float32
-        ),
-        "tile",
-        scatter_dimension=0,
-        tiled=True,
+        )
     )
     act1 = jnp.tanh(first_pre + b_in[:, None]).astype(jnp.bfloat16)
-    middle_pre = lax.psum_scatter(column_term(w_mid, act1), "tile", scatter_dimension=0, tiled=True)
+    middle_pre = scatter_sum(column_term(w_mid, act1))
     act2 = jnp.tanh(middle_pre + b_mid[:, None]).astype(jnp.bfloat16)
     pre3 = (
-        lax.psum_scatter(column_term(w_out, act2), "tile", scatter_dimension=0, tiled=True)
+        scatter_sum(column_term(w_out, act2))
         + b_out[:, None]
     )
     rates = 0.5 * jax.nn.softplus(pre3)
@@ -130,17 +141,17 @@
     )
     g3 = (well_grad * 0.5 * jax.nn.sigmoid(pre3)).astype(jnp.bfloat16)
     g_b_out = jnp.sum(g3.astype(jnp.float32), axis=1)
-    g_act2, g_w_out = back_step(w_out, act2, lax.all_gather(g3, "tile", axis=0, tiled=True))
+    g_act2, g_w_out = back_step(w_out, act2, gather(g3))
     act2_f = act2.astype(jnp.float32)
     g2 = (g_act2 * (1.0 - act2_f * act2_f)).astype(jnp.bfloat16)
     g_b_mid = jnp.sum(g2.astype(jnp.float32), axis=1)
-    g_act1, g_w_mid = back_step(w_mid, act1, lax.all_gather(g2, "tile", axis=0, tiled=True))
+    g_act1, g_w_mid = back_step(w_mid, act1, gather(g2))
     act1_f = act1.astype(jnp.float32)
     g1 = (g_act1 * (1.0 - act1_f * act1_f)).astype(jnp.bfloat16)
     g_b_in = jnp.sum(g1.astype(jnp.float32), axis=1)
     g_w_in = lax.dot_general(
         observed,
-        lax.all_gather(g1, "tile", axis=0, tiled=True),
+        gather(g1),
         (((0,), (1,)), ((), ())),
         preferred_element_type=jnp.float32,
     )

time: 2200 us -> 363 us (0.17)
  waiting for transfers between devices: 1510 us -> 108 us
  blocking collectives: 611 us -> 148 us
  starting transfers between devices: 30.4 us -> 57.9 us
    reduce_scatter x2 -> x0, waiting for transfers between devices: 710 us -> none  [the longest x1 375 us: per_device(): lax.psum_scatter(column_term(w_mid, act1), 'tile', scatter_dimension=0, t...]
    unnamed x5 -> x1, waiting for transfers between devices: 692 us -> 0.02 us
    all_gather x3 -> x0, blocking collectives: 489 us -> none  [the longest x1 169 us: per_device(): lax.all_gather(g3, 'tile', axis=0, tiled=True)]
    all_to_all x0 -> x3, blocking collectives: none -> 120 us  [the longest x2 78.5 us: gather(): got = lax.all_to_all(copies, 'tile', 0, 0, tiled=True)]
    psum x1, blocking collectives: 122 us -> 27.7 us  [per_device(): lax.psum((g_w_in, g_b_in, g_w_mid, g_b_mid, g_w_out, g_b_out), 'scen')]
    all_to_all x0 -> x3, waiting for transfers between devices: none -> 51.1 us  [the longest x2 35.5 us: scatter_sum(): parts = lax.all_to_all(parts, 'tile', 0, 0, tiled=True)]
    psum x1, waiting for transfers between devices: 79.5 us -> 33.2 us  [per_device(): lax.psum((g_w_in, g_b_in, g_w_mid, g_b_mid, g_w_out, g_b_out), 'scen')]
    all_to_all x0 -> x3, starting transfers between devices: none -> 22.3 us  [the longest x2 17.7 us: scatter_sum(): parts = lax.all_to_all(parts, 'tile', 0, 0, tiled=True)]
  transfers between devices with their start and end apart: 18 -> 18, of which waited for: 16 -> 16; matrix products, arithmetic and copies ran while one was open for 0% -> 1% of each run, Pallas kernels for 0% -> 0%
where the time goes in v1:
time: 363 us; the launch traced here: 362 us
  blocking collectives  148 us (41%)
  waiting for transfers between devices  108 us (30%)
  starting transfers between devices  57.9 us (16%)
  local copies, waits for them, and re-layouts  15.9 us (4%)
  between operations  14.8 us (4%)
  other arithmetic  8.93 us (2%)
  matrix products  8.43 us (2%)
    all_to_all x2, blocking collectives, gather(): got = lax.all_to_all(copies, 'tile', 0, 0, tiled=True)  78.5 us
    all_to_all x1, blocking collectives, scatter_sum(): parts = lax.all_to_all(parts, 'tile', 0, 0, tiled=True)  41.4 us
    all_to_all x2, waiting for transfers between devices, scatter_sum(): parts = lax.all_to_all(parts, 'tile', 0, 0, tiled=True)  35.5 us
    psum x1, waiting for transfers between devices, per_device(): lax.psum((g_w_in, g_b_in, g_w_mid, g_b_mid, g_w_out, g_b_out), 'scen')  33.2 us
    psum x1, blocking collectives, per_device(): lax.psum((g_w_in, g_b_in, g_w_mid, g_b_mid, g_w_out, g_b_out), 'scen')  27.7 us
    ppermute x7, starting transfers between devices, with_halo(): lax.ppermute(lax.slice_in_dim(block, block.shape[dim] - width, None, axis...  26.5 us
    ppermute x7, waiting for transfers between devices, with_halo(): lax.ppermute(lax.slice_in_dim(block, 0, width, axis=dim), axis, backward)  18.2 us
    all_to_all x2, starting transfers between devices, scatter_sum(): parts = lax.all_to_all(parts, 'tile', 0, 0, tiled=True)  17.7 us
  transfers between devices with their start and end apart: 18, of which 16 were waited for; matrix products, arithmetic and copies ran while one was open for 1% of the time, Pallas kernels for 0%

profile of v1, /device:TPU:1, one launch (start us, length us, event | category | flops | bytes accessed | tf_op | source)
XLA Modules:
  0.0 361.7 jit_solution(12480633515029646144)
XLA Ops:
  10.7 41.4 %all_to_all.30 = f32[64,32,128]{2,1,0:T(8,128)S(1)} all-to-all(f32[64,32,128]{2,1,0:T(8,128)S(1)} %bitcast.72), channel_id=1, replica_groups=mesh['scen'=4,'tile'=64] {'tile'}, dimensions={0} | all-to-all | bytes 2097152 | tf_op jit(solution)/shard_map/all_to_all | solution.py:36
  53.9 9.3 %all-to-all-start.1 = ((f32[64,32,128]{2,1,0:T(8,128)}), f32[64,32,128]{2,1,0:T(8,128)S(1)}, u32[]{:S(2)}, u32[]{:S(2)}) async-start(f32[64,32,128]{2,1,0:T(8,128)} %bitcast.4), calls=%async_computation.1 | async-start | bytes 2097152 | tf_op jit(solution)/shard_map/all_to_all | solution.py:36
  63.7 2.9 collective-permute-start
  67.9 23.8 %all-to-all-done.1 = f32[64,32,128]{2,1,0:T(8,128)S(1)} async-done(((f32[64,32,128]{2,1,0:T(8,128)}), f32[64,32,128]{2,1,0:T(8,128)S(1)}, u32[]{:S(2)}, u32[]{:S(2)}) %all-to-all-start.1) | async-done | bytes 1048608 | tf_op jit(solution)/shard_map/all_to_all | solution.py:36
  93.0 8.4 %all-to-all-start.2 = ((f32[64,8,128]{2,1,0:T(8,128)}), f32[64,8,128]{2,1,0:T(8,128)S(1)}, u32[]{:S(2)}, u32[]{:S(2)}) async-start(f32[64,8,128]{2,1,0:T(8,128)} %bitcast.6), calls=%async_computation.2 | async-start | bytes 524288 | tf_op jit(solution)/shard_map/all_to_all | solution.py:36
  101.8 11.7 %all-to-all-done.2 = f32[64,8,128]{2,1,0:T(8,128)S(1)} async-done(((f32[64,8,128]{2,1,0:T(8,128)}), f32[64,8,128]{2,1,0:T(8,128)S(1)}, u32[]{:S(2)}, u32[]{:S(2)}) %all-to-all-start.2) | async-done | bytes 262176 | tf_op jit(solution)/shard_map/all_to_all | solution.py:36
  115.5 2.4 collective-permute-start.2
  119.9 3.8 %collective-permute-done.3 = bf16[128,1,512]{0,2,1:T(8,128)(2,1)S(1)} collective-permute-done((bf16[128,1,512]{0,2,1:T(8,128)(2,1)S(1)}, bf16[128,1,512]{0,2,1:T(8,128)(2,1)S(1)}, u32[]{:S(2)}, u32[]{:S(2)}) %collective-permute-start.3) | collective-permute-done | bytes 131104 | tf_op jit(solution)/shard_map/ppermute | solution.py:17
  124.7 3.0 collective-permute-start.4
  129.6 3.8 %collective-permute-done.5 = bf16[128,1,512]{0,2,1:T(8,128)(2,1)S(1)} collective-permute-done((bf16[128,1,512]{0,2,1:T(8,128)(2,1)S(1)}, bf16[128,1,512]{0,2,1:T(8,128)(2,1)S(1)}, u32[]{:S(2)}, u32[]{:S(2)}) %collective-permute-start.5) | collective-permute-done | bytes 131104 | tf_op jit(solution)/shard_map/ppermute | solution.py:17
  134.4 3.8 %collective-permute-start.6 = (bf16[128,1,512]{0,2,1:T(8,128)(2,1)S(1)}, bf16[128,1,512]{0,2,1:T(8,128)(2,1)S(1)}, u32[]{:S(2)}, u32[]{:S(2)}) collective-permute-start(bf16[128,1,512]{0,2,1:T(8,128)(2,1)S(1)} %get-tuple-element.23), channel_id=1, source_target_pairs={{0,1},{1,2},{2,3},{3,4},{4,5},{5,6},{6,7},{7,8},{8,9},{9,10},{10,1... | collective-permute-start | bytes 393224 | tf_op jit(solution)/shard_map/ppermute | solution.py:14
  140.1 3.8 %collective-permute-done.7 = bf16[128,1,512]{0,2,1:T(8,128)(2,1)S(1)} collective-permute-done((bf16[128,1,512]{0,2,1:T(8,128)(2,1)S(1)}, bf16[128,1,512]{0,2,1:T(8,128)(2,1)S(1)}, u32[]{:S(2)}, u32[]{:S(2)}) %collective-permute-start.7) | collective-permute-done | bytes 131104 | tf_op jit(solution)/shard_map/ppermute | solution.py:17
  146.6 3.7 %collective-permute-start.9 = (f32[128,1,512]{0,2,1:T(8,128)S(1)}, f32[128,1,512]{0,2,1:T(8,128)S(1)}, u32[]{:S(2)}, u32[]{:S(2)}) collective-permute-start(f32[128,1,512]{0,2,1:T(8,128)S(1)} %get-tuple-element.21), channel_id=1, source_target_pairs={{0,1},{1,2},{2,3},{3,4},{4,5},{5,6},{6,7},{7,8},{8,9},{9,10},{10,1... | collective-permute-start | bytes 786440 | tf_op jit(solution)/shard_map/ppermute | solution.py:14
  153.6 3.8 %collective-permute-done.8 = f32[128,1,512]{0,2,1:T(8,128)S(1)} collective-permute-done((f32[128,1,512]{0,2,1:T(8,128)S(1)}, f32[128,1,512]{0,2,1:T(8,128)S(1)}, u32[]{:S(2)}, u32[]{:S(2)}) %collective-permute-start.8) | collective-permute-done | bytes 262176 | tf_op jit(solution)/shard_map/ppermute | solution.py:17
  160.5 5.4 %collective-permute-start.11 = (f32[128,1,512]{2,0,1:T(8,128)S(1)}, f32[128,1,512]{2,0,1:T(8,128)}, u32[]{:S(2)}, u32[]{:S(2)}) collective-permute-start(f32[128,1,512]{2,0,1:T(8,128)S(1)} %copy.54), channel_id=1, source_target_pairs={{0,1},{1,2},{2,3},{3,4},{4,5},{5,6},{6,7},{7,8},{8,9},{9,10},{10,1... | collective-permute-start | bytes 786440 | tf_op jit(solution)/shard_map/ppermute | solution.py:14
  165.9 2.0 collective-permute-done.10
  170.9 2.4 broadcast_multiply_fusion
  174.8 5.3 %collective-permute-start.13 = (f32[128,1,512]{2,0,1:T(8,128)S(1)}, f32[128,1,512]{2,0,1:T(8,128)}, u32[]{:S(2)}, u32[]{:S(2)}) collective-permute-start(f32[128,1,512]{2,0,1:T(8,128)S(1)} %copy.60), channel_id=1, source_target_pairs={{0,1},{1,2},{2,3},{3,4},{4,5},{5,6},{6,7},{7,8},{8,9},{9,10},{10,1... | collective-permute-start | bytes 786440 | tf_op jit(solution)/shard_map/ppermute | solution.py:14
  186.6 59.9 %all_to_all.31 = bf16[64,8,128]{2,1,0:T(8,128)(2,1)S(1)} all-to-all(bf16[64,8,128]{2,1,0:T(8,128)(2,1)S(1)} %broadcast_in_dim.6), channel_id=1, replica_groups=mesh['scen'=4,'tile'=64] {'tile'}, dimensions={0} | all-to-all | bytes 262144 | tf_op jit(solution)/shard_map/all_to_all | solution.py:43
  246.8 18.6 %all_to_all.32 = bf16[64,32,128]{2,1,0:T(8,128)(2,1)S(1)} all-to-all(bf16[64,32,128]{2,1,0:T(8,128)(2,1)S(1)} %broadcast_in_dim.7), channel_id=1, replica_groups=mesh['scen'=4,'tile'=64] {'tile'}, dimensions={0} | all-to-all | bytes 1048576 | tf_op jit(solution)/shard_map/all_to_all | solution.py:43
  266.6 4.6 %all-to-all-start.5 = ((bf16[64,32,128]{2,1,0:T(8,128)(2,1)}), bf16[64,32,128]{2,1,0:T(8,128)(2,1)S(1)}, u32[]{:S(2)}, u32[]{:S(2)}) async-start(bf16[64,32,128]{2,1,0:T(8,128)(2,1)} %broadcast_in_dim.8), calls=%async_computation.5 | async-start | bytes 1048576 | tf_op jit(solution)/shard_map/all_to_all | solution.py:43
  273.1 15.6 %all-to-all-done.5 = bf16[64,32,128]{2,1,0:T(8,128)(2,1)S(1)} async-done(((bf16[64,32,128]{2,1,0:T(8,128)(2,1)}), bf16[64,32,128]{2,1,0:T(8,128)(2,1)S(1)}, u32[]{:S(2)}, u32[]{:S(2)}) %all-to-all-start.5) | async-done | bytes 524320 | tf_op jit(solution)/shard_map/all_to_all | solution.py:43
  289.8 27.7 %all-reduce.7 = (f32[32]{0:T(128)}, f32[32]{0:T(128)}, f32[8]{0:T(128)}) all-reduce(f32[32]{0:T(128)S(1)} %get-tuple-element.35, f32[32]{0:T(128)S(1)} %get-tuple-element.37, f32[8]{0:T(128)S(1)} %get-tuple-element.39), channel_id=1, replica_groups=mesh['scen'=4,'tile'=64] {'scen'}, use_global_device_ids=true, to_apply=%region_5.6 | all-reduce | flops 72 | bytes 576 | tf_op jit(solution)/shard_map/psum | solution.py:158
  317.5 33.2 %all-reduce.11.cloned.1.call-done = (f32[64,2048]{1,0:T(8,128)}, f32[32,2048]{1,0:T(8,128)}, f32[32,512]{1,0:T(8,128)}) async-done(((f32[64,2048]{1,0:T(8,128)}, f32[32,2048]{1,0:T(8,128)}, f32[32,512]{1,0:T(8,128)}), (f32[64,2048]{1,0:T(8,128)}, f32[32,2048]{1,0:T(8,128)}, f32[32,512]{1,0:T(8,128)})) %all-reduce.11.cloned.1.call-update) | async-done | bytes 851984 | tf_op jit(solution)/shard_map/psum | solution.py:158
  (138 shorter events, 46.7 us)
Async XLA Ops:
  10.6 41.5 %copy-start.26 = (f32[32]{0:T(128)S(1)}, f32[32]{0:T(128)}, u32[]{:S(2)}) copy-start(f32[32]{0:T(128)} %param.23) | copy-start | bytes 388
  10.7 41.6 %copy-start.7 = (bf16[32,2048]{1,0:T(8,128)(2,1)S(1)}, bf16[32,2048]{1,0:T(8,128)(2,1)}, u32[]{:S(2)}) copy-start(bf16[32,2048]{1,0:T(8,128)(2,1)} %param.24) | copy-start | bytes 393220
  53.9 37.8 %all-to-all-start.1 = ((f32[64,32,128]{2,1,0:T(8,128)}), f32[64,32,128]{2,1,0:T(8,128)S(1)}, u32[]{:S(2)}, u32[]{:S(2)}) async-start(f32[64,32,128]{2,1,0:T(8,128)} %bitcast.4), calls=%async_computation.1 | async-start | bytes 2097152 | tf_op jit(solution)/shard_map/all_to_all | solution.py:36
  63.6 37.7 %copy-start.28 = (f32[8,4]{0,1:T(4,128)S(1)}, f32[8,4]{0,1:T(4,128)}, u32[]{:S(2)}) copy-start(f32[8,4]{0,1:T(4,128)} %param.17) | copy-start | bytes 388
  63.6 37.7 %copy-start.29 = (s32[128]{0:T(128)S(1)}, s32[128]{0:T(128)}, u32[]{:S(2)}) copy-start(s32[128]{0:T(128)} %param.18) | copy-start | bytes 1540
  63.7 38.0 %collective-permute-start = (bf16[128,1,512]{0,2,1:T(8,128)(2,1)S(1)}, bf16[128,1,512]{0,2,1:T(8,128)(2,1)S(1)}, u32[]{:S(2)}, u32[]{:S(2)}) collective-permute-start(bf16[128,1,512]{0,2,1:T(8,128)(2,1)S(1)} %get-tuple-element.29), channel_id=1, source_target_pairs={{0,1},{1,2},{2,3},{3,4},{4,5},{5,6},{6,7},{7,8},{8,9},{9,10},{10,1... | collective-permute-start | bytes 393224 | tf_op jit(solution)/shard_map/ppermute | solution.py:14
  66.6 35.1 %collective-permute-start.1 = (bf16[128,1,512]{0,2,1:T(8,128)(2,1)S(1)}, bf16[128,1,512]{0,2,1:T(8,128)(2,1)S(1)}, u32[]{:S(2)}, u32[]{:S(2)}) collective-permute-start(bf16[128,1,512]{0,2,1:T(8,128)(2,1)S(1)} %get-tuple-element.30), channel_id=1, source_target_pairs={{1,0},{2,1},{3,2},{4,3},{5,4},{6,5},{7,6},{8,7},{9,8},{10,9},{11,1... | collective-permute-start | bytes 393224 | tf_op jit(solution)/shard_map/ppermute | solution.py:17
  93.0 20.5 %all-to-all-start.2 = ((f32[64,8,128]{2,1,0:T(8,128)}), f32[64,8,128]{2,1,0:T(8,128)S(1)}, u32[]{:S(2)}, u32[]{:S(2)}) async-start(f32[64,8,128]{2,1,0:T(8,128)} %bitcast.6), calls=%async_computation.2 | async-start | bytes 524288 | tf_op jit(solution)/shard_map/all_to_all | solution.py:36
  115.5 4.4 %collective-permute-start.2 = (bf16[128,1,512]{0,2,1:T(8,128)(2,1)S(1)}, bf16[128,1,512]{0,2,1:T(8,128)(2,1)S(1)}, u32[]{:S(2)}, u32[]{:S(2)}) collective-permute-start(bf16[128,1,512]{0,2,1:T(8,128)(2,1)S(1)} %get-tuple-element.27), channel_id=1, source_target_pairs={{0,1},{1,2},{2,3},{3,4},{4,5},{5,6},{6,7},{7,8},{8,9},{9,10},{10,1... | collective-permute-start | bytes 393224 | tf_op jit(solution)/shard_map/ppermute | solution.py:14
  118.0 5.7 %collective-permute-start.3 = (bf16[128,1,512]{0,2,1:T(8,128)(2,1)S(1)}, bf16[128,1,512]{0,2,1:T(8,128)(2,1)S(1)}, u32[]{:S(2)}, u32[]{:S(2)}) collective-permute-start(bf16[128,1,512]{0,2,1:T(8,128)(2,1)S(1)} %get-tuple-element.28), channel_id=1, source_target_pairs={{1,0},{2,1},{3,2},{4,3},{5,4},{6,5},{7,6},{8,7},{9,8},{10,9},{11,1... | collective-permute-start | bytes 393224 | tf_op jit(solution)/shard_map/ppermute | solution.py:17
  124.7 5.0 %collective-permute-start.4 = (bf16[128,1,512]{0,2,1:T(8,128)(2,1)S(1)}, bf16[128,1,512]{0,2,1:T(8,128)(2,1)S(1)}, u32[]{:S(2)}, u32[]{:S(2)}) collective-permute-start(bf16[128,1,512]{0,2,1:T(8,128)(2,1)S(1)} %get-tuple-element.25), channel_id=1, source_target_pairs={{0,1},{1,2},{2,3},{3,4},{4,5},{5,6},{6,7},{7,8},{8,9},{9,10},{10,1... | collective-permute-start | bytes 393224 | tf_op jit(solution)/shard_map/ppermute | solution.py:14
  127.7 5.7 %collective-permute-start.5 = (bf16[128,1,512]{0,2,1:T(8,128)(2,1)S(1)}, bf16[128,1,512]{0,2,1:T(8,128)(2,1)S(1)}, u32[]{:S(2)}, u32[]{:S(2)}) collective-permute-start(bf16[128,1,512]{0,2,1:T(8,128)(2,1)S(1)} %get-tuple-element.26), channel_id=1, source_target_pairs={{1,0},{2,1},{3,2},{4,3},{5,4},{6,5},{7,6},{8,7},{9,8},{10,9},{11,1... | collective-permute-start | bytes 393224 | tf_op jit(solution)/shard_map/ppermute | solution.py:17
  134.4 5.7 %collective-permute-start.6 = (bf16[128,1,512]{0,2,1:T(8,128)(2,1)S(1)}, bf16[128,1,512]{0,2,1:T(8,128)(2,1)S(1)}, u32[]{:S(2)}, u32[]{:S(2)}) collective-permute-start(bf16[128,1,512]{0,2,1:T(8,128)(2,1)S(1)} %get-tuple-element.23), channel_id=1, source_target_pairs={{0,1},{1,2},{2,3},{3,4},{4,5},{5,6},{6,7},{7,8},{8,9},{9,10},{10,1... | collective-permute-start | bytes 393224 | tf_op jit(solution)/shard_map/ppermute | solution.py:14
  138.1 5.7 %collective-permute-start.7 = (bf16[128,1,512]{0,2,1:T(8,128)(2,1)S(1)}, bf16[128,1,512]{0,2,1:T(8,128)(2,1)S(1)}, u32[]{:S(2)}, u32[]{:S(2)}) collective-permute-start(bf16[128,1,512]{0,2,1:T(8,128)(2,1)S(1)} %get-tuple-element.24), channel_id=1, source_target_pairs={{1,0},{2,1},{3,2},{4,3},{5,4},{6,5},{7,6},{8,7},{9,8},{10,9},{11,1... | collective-permute-start | bytes 393224 | tf_op jit(solution)/shard_map/ppermute | solution.py:17
  146.6 7.0 %collective-permute-start.9 = (f32[128,1,512]{0,2,1:T(8,128)S(1)}, f32[128,1,512]{0,2,1:T(8,128)S(1)}, u32[]{:S(2)}, u32[]{:S(2)}) collective-permute-start(f32[128,1,512]{0,2,1:T(8,128)S(1)} %get-tuple-element.21), channel_id=1, source_target_pairs={{0,1},{1,2},{2,3},{3,4},{4,5},{5,6},{6,7},{7,8},{8,9},{9,10},{10,1... | collective-permute-start | bytes 786440 | tf_op jit(solution)/shard_map/ppermute | solution.py:14
  150.3 7.1 %collective-permute-start.8 = (f32[128,1,512]{0,2,1:T(8,128)S(1)}, f32[128,1,512]{0,2,1:T(8,128)S(1)}, u32[]{:S(2)}, u32[]{:S(2)}) collective-permute-start(f32[128,1,512]{0,2,1:T(8,128)S(1)} %get-tuple-element.22), channel_id=1, source_target_pairs={{1,0},{2,1},{3,2},{4,3},{5,4},{6,5},{7,6},{8,7},{9,8},{10,9},{11,1... | collective-permute-start | bytes 786440 | tf_op jit(solution)/shard_map/ppermute | solution.py:17
  159.1 8.8 %collective-permute-start.10 = (f32[128,1,512]{2,0,1:T(8,128)S(1)}, f32[128,1,512]{2,0,1:T(8,128)S(1)}, u32[]{:S(2)}, u32[]{:S(2)}) collective-permute-start(f32[128,1,512]{2,0,1:T(8,128)S(1)} %copy.52), channel_id=1, source_target_pairs={{1,0},{2,1},{3,2},{4,3},{5,4},{6,5},{7,6},{8,7},{9,8},{10,9},{11,1... | collective-permute-start | bytes 786440 | tf_op jit(solution)/shard_map/ppermute | solution.py:17
  160.5 8.0 %collective-permute-start.11 = (f32[128,1,512]{2,0,1:T(8,128)S(1)}, f32[128,1,512]{2,0,1:T(8,128)}, u32[]{:S(2)}, u32[]{:S(2)}) collective-permute-start(f32[128,1,512]{2,0,1:T(8,128)S(1)} %copy.54), channel_id=1, source_target_pairs={{0,1},{1,2},{2,3},{3,4},{4,5},{5,6},{6,7},{7,8},{8,9},{9,10},{10,1... | collective-permute-start | bytes 786440 | tf_op jit(solution)/shard_map/ppermute | solution.py:14
  173.4 7.7 %collective-permute-start.12 = (f32[128,1,512]{2,0,1:T(8,128)S(1)}, f32[128,1,512]{2,0,1:T(8,128)S(1)}, u32[]{:S(2)}, u32[]{:S(2)}) collective-permute-start(f32[128,1,512]{2,0,1:T(8,128)S(1)} %copy.58), channel_id=1, source_target_pairs={{1,0},{2,1},{3,2},{4,3},{5,4},{6,5},{7,6},{8,7},{9,8},{10,9},{11,1... | collective-permute-start | bytes 786440 | tf_op jit(solution)/shard_map/ppermute | solution.py:17
  174.8 7.9 %collective-permute-start.13 = (f32[128,1,512]{2,0,1:T(8,128)S(1)}, f32[128,1,512]{2,0,1:T(8,128)}, u32[]{:S(2)}, u32[]{:S(2)}) collective-permute-start(f32[128,1,512]{2,0,1:T(8,128)S(1)} %copy.60), channel_id=1, source_target_pairs={{0,1},{1,2},{2,3},{3,4},{4,5},{5,6},{6,7},{7,8},{8,9},{9,10},{10,1... | collective-permute-start | bytes 786440 | tf_op jit(solution)/shard_map/ppermute | solution.py:14
  185.3 61.2 %copy-start.11 = (bf16[32,128]{1,0:T(8,128)(2,1)S(1)}, bf16[32,128]{1,0:T(8,128)(2,1)}, u32[]{:S(2)}) copy-start(bf16[32,128]{1,0:T(8,128)(2,1)} %copy-done.10) | copy-start | bytes 24580
  185.3 61.2 %copy-start.13 = (bf16[32,512]{1,0:T(8,128)(2,1)S(1)}, bf16[32,512]{1,0:T(8,128)(2,1)}, u32[]{:S(2)}) copy-start(bf16[32,512]{1,0:T(8,128)(2,1)} %param.26) | copy-start | bytes 98308
  266.6 22.0 %all-to-all-start.5 = ((bf16[64,32,128]{2,1,0:T(8,128)(2,1)}), bf16[64,32,128]{2,1,0:T(8,128)(2,1)S(1)}, u32[]{:S(2)}, u32[]{:S(2)}) async-start(bf16[64,32,128]{2,1,0:T(8,128)(2,1)} %broadcast_in_dim.8), calls=%async_computation.5 | async-start | bytes 1048576 | tf_op jit(solution)/shard_map/all_to_all | solution.py:43
  271.3 79.4 %all-reduce.11.cloned.1.call-start = ((), (), s32[]{:S(2)}) async-start(), calls=%async_computation.6 | async-start | bytes 1703936 | tf_op jit(solution)/shard_map/psum | solution.py:158
  (24 other events, 187.8 us)
Sparse Core Ops, SparseCore 0:
  289.9 60.7 all-reduce.10

commit v2 on v0

v2 whole, which is shorter than its diff:
```python
import math

import jax
import jax.numpy as jnp
from jax import lax
from jax.experimental import pallas as pl
from jax.experimental.pallas import tpu as pltpu
from jax.sharding import PartitionSpec as P

BF = jnp.bfloat16
F32 = jnp.float32
HIGH = lax.Precision.HIGHEST
TILES = 64
SCENS = 4
STRIDES = {"zh": 16, "x": 4, "y": 1}


def dot(left, right, contract, precision=None):
    return lax.dot_general(
        left, right, (contract, ((), ())), precision=precision, preferred_element_type=F32
    )


def position(axis):
    return (lax.axis_index("tile") // STRIDES[axis]) % 4


def from_ahead(block, axis, ahead):
    stride = STRIDES[axis]
    pairs = []
    for target in range(TILES):
        mine = target // stride % 4
        pairs.append((target + ((mine + ahead) % 4 - mine) * stride, target))
    return lax.ppermute(block, "tile", pairs)


def pieces(block, axis):
    return [block] + [from_ahead(block, axis, ahead) for ahead in (1, 2, 3)]


def place(blocks, axis, dim):
    shape = list(blocks[0].shape)
    shape[dim] *= 4
    whole = jnp.zeros(shape, blocks[0].dtype)
    mine = position(axis)
    for ahead, block in enumerate(blocks):
        start = ((mine + ahead) % 4) * block.shape[dim]
        whole = lax.dynamic_update_slice_in_dim(whole, block, start, axis=dim)
    return whole


def exchange(parts):
    return lax.all_to_all(parts, "tile", 0, 0, tiled=True)


def to_all(block):
    return exchange(jnp.broadcast_to(block[None], (TILES,) + block.shape))


CHUNK = 16
ROW_SETS = (
    ((0, 4), (1, 5), (2, 6), (3, 7), (4, 8)),
    ((4, 8), (3, 9), (2, 10), (3, 9), (4, 8)),
    ((8, 12), (7, 11), (6, 10), (5, 9), (4, 8)),
)


def spread_kernel(diff_ref, recharge_ref, cells_ref, high_ref, low_ref, sum_ref, charge_ref):
    width = diff_ref.shape[1]
    column = lax.broadcasted_iota(jnp.int32, (CHUNK, width), 1)
    lane = lax.broadcasted_iota(jnp.int32, (CHUNK, 128), 1)
    for part in range(3):
        sets = ROW_SETS[part]

        def chunk(index, carry, part=part, sets=sets):
            at = pl.multiple_of(part * 64 + index * CHUNK, CHUNK)
            cells = cells_ref[pl.ds(at, CHUNK), :]
            own_row = cells >> 9
            hit = column == (cells & (width - 1))
            values = {
                row: jnp.where(hit & (own_row == row - 4 * part), 1.0, 0.0)
                for row in range(*sets[0])
            }
            sums = {}
            charge = jnp.zeros((CHUNK, 128), F32)
            for step in range(5):
                if step < 4:
                    product = None
                    for row in range(4, 8):
                        if row in values:
                            v = values[row]
                            sums[row] = sums[row] + v if row in sums else v
                            term = v * recharge_ref[row - 4 : row - 3, :]
                            product = term if product is None else product + term
                    if product is not None:
                        total = jnp.sum(product, axis=1, keepdims=True)
                        charge = jnp.where(lane == step, total, charge)
                    weighted = {row: v * diff_ref[row : row + 1, :] for row, v in values.items()}
                    later = {}
                    for row in range(*sets[step + 1]):
                        out = values.get(row)
                        if row in weighted:
                            w = weighted[row]
                            left = jnp.where(column == 0, 0.0, pltpu.roll(w, 1, 1))
                            right = jnp.where(column == width - 1, 0.0, pltpu.roll(w, width - 1, 1))
                            out = out + (left + right - 4.0 * w)
                        for near in (row - 1, row + 1):
                            if near in weighted:
                                out = weighted[near] if out is None else out + weighted[near]
                        later[row] = out
                    values = later
            for row in range(4, 8):
                columns = slice((row - 4) * width, (row - 3) * width)
                v = values[row]
                high = v.astype(BF)
                high_ref[pl.ds(at, CHUNK), columns] = high
                low_ref[pl.ds(at, CHUNK), columns] = (v - high.astype(F32)).astype(BF)
                sum_ref[pl.ds(at, CHUNK), columns] = sums.get(row, jnp.zeros_like(v))
            charge_ref[pl.ds(at, CHUNK), :] = charge
            return carry

        lax.fori_loop(0, 64 // CHUNK, chunk, 0)


def spread_operator(diffusivity, recharge_map, cells):
    monitors = cells.shape[0]
    flat = recharge_map.shape[0] * recharge_map.shape[1]
    return pl.pallas_call(
        spread_kernel,
        out_shape=(
            jax.ShapeDtypeStruct((monitors, flat), BF),
            jax.ShapeDtypeStruct((monitors, flat), BF),
            jax.ShapeDtypeStruct((monitors, flat), F32),
            jax.ShapeDtypeStruct((monitors, 128), F32),
        ),
        compiler_params=pltpu.CompilerParams(vmem_limit_bytes=24 * 1024 * 1024),
        cost_estimate=pl.CostEstimate(
            flops=30_000_000, bytes_accessed=4_000_000, transcendentals=0
        ),
    )(diffusivity, recharge_map, cells)


def per_device(
    initial_heads,
    diffusivity,
    recharge_map,
    rate_table,
    recharge_ids,
    monitor_cells,
    well_cells,
    targets,
    w_in,
    b_in,
    w_mid,
    b_mid,
    w_out,
    b_out,
):
    members, rows, cols = initial_heads.shape
    cells = rows * cols
    scen = lax.axis_index("scen")
    tile = lax.axis_index("tile")
    positions = jnp.arange(cells, dtype=jnp.int32)
    heads = initial_heads.reshape(members, cells)

    with jax.named_scope("first_layer"):
        monitor_pick = (monitor_cells[:, None] == positions[None, :]).astype(BF)
        observed = dot(heads, monitor_pick, ((1,), (1,))).astype(BF)
        first_terms = dot(observed, w_in, ((1,), (0,))).astype(BF)
        first_terms = exchange(first_terms.reshape(TILES, 32, 128))

    with jax.named_scope("biases"):
        small = jnp.zeros((8, 128), F32)
        small = small.at[0, :72].set(jnp.concatenate([b_in, b_mid, b_out]))
        small = small.at[1, :64].set(targets)
        small = to_all(small)
        b_in_all = small[:, 0, :32].reshape(2048)
        b_mid_all = small[:, 0, 32:64].reshape(2048)
        b_out_all = small[:, 0, 64:72].reshape(512)
        targets_all = small[:, 1, :64]

    with jax.named_scope("weights"):
        mid = lax.dynamic_slice_in_dim(w_mid, scen * 512, 512, axis=1)
        mid = place(pieces(mid[None], "zh"), "zh", 0)
        mid = place(pieces(mid[:, None], "y"), "y", 1).reshape(512, 512)
        mids = pieces(mid, "x")
        swap = []
        for s in range(SCENS):
            for z in range(4):
                for r in range(16):
                    swap.append((z * TILES + s * 16 + r, s * TILES + z * 16 + r))
        last = lax.ppermute(w_out, ("scen", "tile"), swap)
        last = place(pieces(last, "y"), "y", 0)
        last = place(pieces(last, "x"), "x", 0)

    with jax.named_scope("operator"):
        slab = jnp.concatenate(
            [diffusivity, jnp.pad((monitor_cells + 1).astype(F32), (0, cols - 64))[None]], axis=0
        )
        down = [(i, i + 1) for i in range(TILES - 1)]
        before = lax.ppermute(slab, "tile", down)
        after = lax.ppermute(slab, "tile", [(b, a) for a, b in down])
        near_cells = jnp.concatenate([before[4, :64], slab[4, :64], after[4, :64]])
        near_cells = near_cells.astype(jnp.int32) - 1
        near_diff = jnp.concatenate([before[:4], diffusivity, after[:4]], axis=0)
        high, low, summed, charge = spread_operator(near_diff, recharge_map, near_cells[:, None])
        well_hot = (well_cells[:, None] == positions[None, :]).astype(F32)
        coupling = dot(well_hot, summed, ((1,), (1,)), HIGH)
        codes = jnp.arange(rate_table.shape[0], dtype=jnp.int32)
        pattern_hot = (recharge_ids[:, None] == codes[None, :]).astype(F32)
        monthly = dot(pattern_hot, rate_table, ((1,), (0,)), HIGH)
        backward_charge = jnp.stack([charge[:, 3], charge[:, 2], charge[:, 1], charge[:, 0]])
        still = (
            dot(heads, high, ((1,), (1,)))
            + dot(heads, low, ((1,), (1,)))
            + dot(monthly, backward_charge, ((1,), (0,)), HIGH)
        )
        still = still.reshape(TILES, 2, 3, 64).transpose(0, 2, 1, 3).reshape(TILES, 3, 128)
        coupling = coupling.reshape(8, 3, 64).transpose(1, 0, 2).reshape(12, 128)
        sent = jnp.concatenate(
            [
                still,
                jnp.broadcast_to(coupling[None], (TILES, 12, 128)),
                jnp.zeros((TILES, 1, 128), F32),
            ],
            axis=1,
        )
        got = exchange(sent)
        none = jnp.zeros((1, 128), F32)
        still = (
            got[:, 1]
            + jnp.concatenate([none, got[:-1, 2]], axis=0)
            + jnp.concatenate([got[1:, 0], none], axis=0)
        )
        coupling = got[:, 3:15].reshape(TILES, 3, 8, 64).transpose(0, 2, 1, 3).reshape(512, 192)

    with jax.named_scope("act1"):
        first_pre = jnp.sum(first_terms.astype(F32), axis=0)
        act1 = jnp.tanh(first_pre.reshape(2, 2048) + b_in_all[None, :]).astype(BF)
        shared = jnp.concatenate([act1.reshape(32, 128), observed.reshape(TILES, 128)], axis=0)
        shared = lax.all_gather(shared, "scen", axis=0, tiled=False)
        act1 = shared[:, :32].reshape(8, 2048)
        observed_all = shared[:, 32:].reshape(SCENS, TILES, 2, 64).transpose(1, 0, 2, 3)
        observed_all = observed_all.reshape(512, 64)

    with jax.named_scope("act2"):
        here = position("x")
        act1_x = act1.reshape(8, 4, 4, 128)
        middle_pre = lax.dynamic_slice_in_dim(b_mid_all, scen * 512, 512)[None, :]
        for ahead in range(4):
            part = lax.dynamic_slice_in_dim(act1_x, (here + ahead) % 4, 1, axis=2)
            middle_pre = middle_pre + dot(part.reshape(8, 512), mids[ahead], ((1,), (0,)))
        act2 = jnp.tanh(middle_pre).astype(BF)

    with jax.named_scope("pre3"):
        terms = dot(act2, last, ((1,), (0,)))
        shared = jnp.concatenate(
            [terms.reshape(32, 128), act2.astype(F32).reshape(32, 128), still], axis=0
        )
        shared = lax.all_gather(shared, "scen", axis=0, tiled=False)
        pre3 = jnp.sum(shared[:, :32], axis=0).reshape(8, 512) + b_out_all[None, :]
        act2_all = shared[:, 32:64].reshape(SCENS, 8, 512).astype(BF)
        still = shared[:, 64:].reshape(SCENS, TILES, 2, 64).transpose(1, 0, 2, 3)
        still = still.reshape(TILES, 8, 64)

    with jax.named_scope("wells"):
        rates = 0.5 * jax.nn.softplus(pre3)
        owner = lax.broadcasted_iota(jnp.int32, (TILES, 1, 512), 2) // 8
        at_tile = owner == lax.broadcasted_iota(jnp.int32, (TILES, 1, 512), 0)
        by_tile = jnp.where(at_tile, rates[None], 0.0).reshape(512, 512)
        drawn = dot(by_tile, coupling, ((1,), (0,)), HIGH).reshape(TILES, 8, 192)
        blank = jnp.zeros((1, 8, 64), F32)
        sink = (
            drawn[:, :, 64:128]
            + jnp.concatenate([blank, drawn[:-1, :, 128:]], axis=0)
            + jnp.concatenate([drawn[1:, :, :64], blank], axis=0)
        )
        final = (still - sink).astype(BF)
        spread = (final.astype(F32) - targets_all[:, None, :]) / math.sqrt(512)
        wide = jnp.concatenate(
            [
                jnp.concatenate([blank, spread[:-1]], axis=0),
                spread,
                jnp.concatenate([spread[1:], blank], axis=0),
            ],
            axis=2,
        ).reshape(512, 192)
        total = dot(wide, coupling, ((1,), (1,)), HIGH).reshape(TILES, 8, 512)
        total = jnp.sum(jnp.where(at_tile, total, 0.0), axis=0)
        g3 = (-total * 0.5 * jax.nn.sigmoid(pre3)).astype(BF)

    with jax.named_scope("g2"):
        act2_f = act2.astype(F32)
        g2 = (dot(g3, last, ((1,), (1,))) * (1.0 - act2_f * act2_f)).astype(BF)

    with jax.named_scope("regroup"):
        act2_full = act2_all.transpose(1, 0, 2).reshape(8, 2048)
        by_row = jnp.stack([act1, act2_full]).reshape(2, 8, TILES, 32)
        by_row = by_row.transpose(2, 0, 1, 3).reshape(TILES, 4, 128)
        my_final = lax.dynamic_slice_in_dim(final, scen * 2, 2, axis=1).reshape(TILES, 1, 128)
        my_g3 = lax.dynamic_slice_in_dim(g3, scen * 128, 128, axis=1)
        grads = jnp.concatenate([g2.reshape(32, 128), my_g3], axis=0)
        sent = jnp.concatenate(
            [
                jnp.broadcast_to(grads[None], (TILES, 40, 128)),
                by_row,
                my_final,
                jnp.zeros((TILES, 3, 128), BF),
            ],
            axis=1,
        )
        got = exchange(sent)
        final_heads = got[:, 44].reshape(members, 64)

    with jax.named_scope("g1"):
        g1_terms = jnp.zeros((8, 4, 4, 128), F32)
        for ahead in range(4):
            part = dot(g2, mids[ahead], ((1,), (1,))).reshape(8, 4, 1, 128)
            g1_terms = lax.dynamic_update_slice_in_dim(
                g1_terms, part, (here + ahead) % 4, axis=2
            )
        g1_terms = g1_terms.reshape(8, 4, 512).transpose(1, 0, 2)
        g1_terms = lax.all_to_all(g1_terms, "scen", 0, 0, tiled=True)
        act1_f = lax.dynamic_slice_in_dim(act1, scen * 512, 512, axis=1).astype(F32)
        g1 = (jnp.sum(g1_terms, axis=0) * (1.0 - act1_f * act1_f)).astype(BF)
        g1_all = to_all(g1.reshape(32, 128)).reshape(512, 512)

    with jax.named_scope("weight_grads"):
        ones = jnp.ones((512, 8), BF)
        g2_all = got[:, :32].reshape(512, 512)
        g3_all = got[:, 32:40].reshape(512, 128)
        act1_own = jnp.concatenate([got[:, 40:42].reshape(512, 32), ones], axis=1)
        act2_own = jnp.concatenate([got[:, 42:44].reshape(512, 32), ones], axis=1)
        both = jnp.concatenate(
            [dot(act1_own, g2_all, ((0,), (0,))), dot(act2_own, g3_all, ((0,), (0,)))], axis=1
        )
        both = lax.all_gather(both, "scen", axis=0, tiled=False)
        g_w_mid = both[:, :, :512].transpose(1, 0, 2).reshape(40, 2048)
        g_w_out = both[:, :, 512:].transpose(1, 0, 2).reshape(40, 512)
        observed_own = jnp.concatenate([observed_all, ones], axis=1)
        g_w_in = dot(observed_own, g1_all, ((0,), (0,)))
        g_w_in = lax.all_gather(g_w_in, "scen", axis=1, tiled=True)
        g_b_in = lax.dynamic_slice_in_dim(g_w_in[64], tile * 32, 32)
        g_b_mid = lax.dynamic_slice_in_dim(g_w_mid[32], tile * 32, 32)
        g_b_out = lax.dynamic_slice_in_dim(g_w_out[32], tile * 8, 8)
    return (final_heads, g_w_in[:64], g_b_in, g_w_mid[:32], g_b_mid, g_w_out[:32], g_b_out)


def solution(mesh):
    return jax.shard_map(
        per_device,
        mesh=mesh,
        in_specs=(
            P("scen", "tile", None),
            P("tile", None),
            P("tile", None),
            P(),
            P("scen"),
            P("tile"),
            P("tile"),
            P("tile"),
            P("tile", None),
            P("tile"),
            P("tile", None),
            P("tile"),
            P("tile", None),
            P("tile"),
        ),
        out_specs=(
            P("scen", "tile"),
            P("tile", None),
            P("tile"),
            P("tile", None),
            P("tile"),
            P("tile", None),
            P("tile"),
        ),
        check_vma=False,
    )
```

time: 2200 us -> 225 us (0.10)
  waiting for transfers between devices: 1510 us -> 25.5 us
  blocking collectives: 611 us -> 50.5 us
  starting transfers between devices: 30.4 us -> 90.3 us
    reduce_scatter x2 -> x0, waiting for transfers between devices: 710 us -> none  [the longest x1 375 us: per_device(): lax.psum_scatter(column_term(w_mid, act1), 'tile', scatter_dimension=0, t...]
    unnamed x5 -> x0, waiting for transfers between devices: 692 us -> none
    all_gather x3 -> x4, blocking collectives: 489 us -> 50.5 us  [the longest x2 23.1 us: per_device(): shared = lax.all_gather(shared, 'scen', axis=0, tiled=False)]
    psum x1 -> x0, blocking collectives: 122 us -> none  [per_device(): lax.psum((g_w_in, g_b_in, g_w_mid, g_b_mid, g_w_out, g_b_out), 'scen')]
    psum x1 -> x0, waiting for transfers between devices: 79.5 us -> none  [per_device(): lax.psum((g_w_in, g_b_in, g_w_mid, g_b_mid, g_w_out, g_b_out), 'scen')]
    all_to_all x0 -> x6, starting transfers between devices: none -> 49.6 us  [the longest x5 46.2 us: exchange(): return lax.all_to_all(parts, 'tile', 0, 0, tiled=True)]
    all_to_all x0 -> x6, waiting for transfers between devices: none -> 22.5 us  [the longest x5 19.2 us: exchange(): return lax.all_to_all(parts, 'tile', 0, 0, tiled=True)]
  transfers between devices with their start and end apart: 18 -> 24, of which waited for: 16 -> 6; matrix products, arithmetic and copies ran while one was open for 0% -> 14% of each run, Pallas kernels for 0% -> 3%
where the time goes in v2:
time: 225 us; the launch traced here: 223 us
  starting transfers between devices  90.3 us (40%)
  blocking collectives  50.5 us (22%)
  local copies, waits for them, and re-layouts  32.1 us (14%)
  waiting for transfers between devices  25.5 us (11%)
  matrix products  8.35 us (4%)
  other arithmetic  7.88 us (4%)
  Pallas kernels  7 us (3%)
    all_to_all x5, starting transfers between devices, exchange(): return lax.all_to_all(parts, 'tile', 0, 0, tiled=True)  46.2 us
    ppermute x15, starting transfers between devices, from_ahead(): return lax.ppermute(block, 'tile', pairs)  28.4 us
    all_gather x2, blocking collectives, per_device(): shared = lax.all_gather(shared, 'scen', axis=0, tiled=False)  23.1 us
    all_to_all x5, waiting for transfers between devices, exchange(): return lax.all_to_all(parts, 'tile', 0, 0, tiled=True)  19.2 us
    all_gather x1, blocking collectives, per_device(): g_w_in = lax.all_gather(g_w_in, 'scen', axis=1, tiled=True)  17.8 us
    all_gather x1, blocking collectives, per_device(): both = lax.all_gather(both, 'scen', axis=0, tiled=False)  9.65 us
    dot_general x22, matrix products, dot(): lax.dot_general(left, right, (contract, ((), ())), precision=precision, p...  8.35 us
    pallas_call x1, Pallas kernels, spread_operator(): pl.pallas_call(spread_kernel, out_shape=(jax.ShapeDtypeStruct((monitors,...  7 us
  transfers between devices with their start and end apart: 24, of which 6 were waited for; matrix products, arithmetic and copies ran while one was open for 14% of the time, Pallas kernels for 3%

profile of v2, /device:TPU:1, one launch (start us, length us, event | category | flops | bytes accessed | tf_op | source)
XLA Modules:
  0.0 223.5 jit_solution(3607861208530060365)
XLA Ops:
  3.4 4.7 %collective-permute-start.16 = (f32[5,512]{1,0:T(8,128)S(1)}, f32[5,512]{1,0:T(8,128)S(1)}, u32[]{:S(2)}, u32[]{:S(2)}) collective-permute-start(f32[5,512]{1,0:T(8,128)S(1)} %pad_maximum_fusion.4), channel_id=1, source_target_pairs={{0,1},{1,2},{2,3},{3,4},{4,5},{5,6},{6,7},{7,8},{8,9},{9,10},{10,1... | collective-permute-start | bytes 30728 | tf_op jit(solution)/shard_map/operator/ppermute | solution.py:201
  8.8 10.5 %collective-permute-start = (bf16[1,32,512]{2,1,0:T(8,128)(2,1)S(1)}, bf16[1,32,512]{2,1,0:T(8,128)(2,1)S(1)}, u32[]{:S(2)}, u32[]{:S(2)}) collective-permute-start(bf16[1,32,512]{2,1,0:T(8,128)(2,1)S(1)} %dynamic-slice_bitcast_fusion), channel_id=1, source_target_pairs={{16,0},{17,1},{18,2},{19,3},{20,4},{21,5},{22,6},{23,7},{24,8},{25... | collective-permute-start | bytes 98312 | tf_op jit(solution)/shard_map/weights/ppermute | solution.py:34
  19.4 2.1 collective-permute-start.2
  23.7 10.6 %all-to-all-start = ((f32[64,8,128]{2,1,0:T(8,128)}), f32[64,8,128]{2,1,0:T(8,128)S(1)}, u32[]{:S(2)}, u32[]{:S(2)}) async-start(f32[64,8,128]{2,1,0:T(8,128)} %broadcast_in_dim.109), calls=%async_computation | async-start | bytes 524288 | tf_op jit(solution)/shard_map/biases/all_to_all | solution.py:53
  39.4 6.4 %collective-permute-start.9 = (bf16[32,512]{1,0:T(8,128)(2,1)S(1)}, bf16[32,512]{1,0:T(8,128)(2,1)S(1)}, u32[]{:S(2)}, u32[]{:S(2)}) collective-permute-start(bf16[32,512]{1,0:T(8,128)(2,1)S(1)} %copy-done.18), channel_id=1, source_target_pairs={{0,0},{1,1},{2,2},{3,3},{4,4},{5,5},{6,6},{7,7},{8,8},{9,9},{10,10... | collective-permute-start | bytes 98312 | tf_op jit(solution)/shard_map/weights/ppermute | solution.py:192
  46.1 7.0 %operator.1 = (bf16[192,2048]{1,0:T(8,128)(2,1)S(1)}, bf16[192,2048]{1,0:T(8,128)(2,1)S(1)}, f32[192,2048]{1,0:T(8,128)S(1)}, f32[192,128]{1,0:T(8,128)S(1)}) custom-call(f32[12,512]{1,0:T(8,128)S(1)} %pad_maximum_fusion.2.diff_ref, f32[4,512]{1,0:T(4,128)S(1)} %copy-done.1, s32[192,1]{1,0:T(8,128)S(1)} %broadcast_add_fusion.cells_ref), custom_call_target="tpu_custom_call" | custom-call | flops 30000000 | bytes 4000000 | tf_op jit(solution)/shard_map/operator/pallas_call | solution.py:128
  57.1 2.5 %collective-permute-start.3 = (bf16[4,1,32,512]{3,2,1,0:T(8,128)(2,1)S(1)}, bf16[4,1,32,512]{3,2,1,0:T(8,128)(2,1)S(1)}, u32[]{:S(2)}, u32[]{:S(2)}) collective-permute-start(bf16[4,1,32,512]{3,2,1,0:T(8,128)(2,1)S(1)} %bitcast_dynamic-update-slice_fusion), channel_id=1, source_target_pairs={{1,0},{2,1},{3,2},{0,3},{5,4},{6,5},{7,6},{4,7},{9,8},{10,9},{11,1... | collective-permute-start | bytes 393224 | tf_op jit(solution)/shard_map/weights/ppermute | solution.py:34
  60.7 2.1 collective-permute-start.10
  68.0 1.8 collective-permute-done.12
  70.4 2.6 %collective-permute-start.13 = (bf16[128,512]{1,0:T(8,128)(2,1)}, bf16[128,512]{1,0:T(8,128)(2,1)}, u32[]{:S(2)}, u32[]{:S(2)}) collective-permute-start(bf16[128,512]{1,0:T(8,128)(2,1)} %constant_dynamic-update-slice_fusion.4), channel_id=1, source_target_pairs={{4,0},{5,1},{6,2},{7,3},{8,4},{9,5},{10,6},{11,7},{12,8},{13,9},{1... | collective-permute-start | bytes 393224 | tf_op jit(solution)/shard_map/weights/ppermute | solution.py:34
  73.4 10.7 %all-to-all-start.1 = ((bf16[64,32,128]{2,1,0:T(8,128)(2,1)}), bf16[64,32,128]{2,1,0:T(8,128)(2,1)S(1)}, u32[]{:S(2)}, u32[]{:S(2)}) async-start(bf16[64,32,128]{2,1,0:T(8,128)(2,1)} %reshape.360), calls=%async_computation.1 | async-start | bytes 1048576 | tf_op jit(solution)/shard_map/first_layer/all_to_all | solution.py:53
  87.5 1.7 collective-permute-start.7
  97.0 2.0 all-to-all-done.1
  99.8 9.2 %all-to-all-start.2 = ((f32[64,16,128]{2,1,0:T(8,128)}), f32[64,16,128]{2,1,0:T(8,128)S(1)}, u32[]{:S(2)}, u32[]{:S(2)}) async-start(f32[64,16,128]{2,1,0:T(8,128)} %maximum_maximum_fusion.1), calls=%async_computation.2 | async-start | bytes 1048576 | tf_op jit(solution)/shard_map/operator/all_to_all | solution.py:53
  110.2 13.0 %all-gather = bf16[384,128]{1,0:T(8,128)(2,1)S(1)} all-gather(bf16[96,128]{1,0:T(8,128)(2,1)S(1)} %pad_maximum_fusion.3), channel_id=2, replica_groups=mesh['scen'=4,'tile'=64] {'scen'}, dimensions={0}, use_global_device_ids=true | all-gather | bytes 122880 | tf_op jit(solution)/shard_map/act1/all_gather | solution.py:241
  127.7 10.1 %all-gather.1 = f32[512,128]{1,0:T(8,128)S(1)} all-gather(f32[128,128]{1,0:T(8,128)S(1)} %pad_maximum_fusion.1), channel_id=3, replica_groups=mesh['scen'=4,'tile'=64] {'scen'}, dimensions={0}, use_global_device_ids=true | all-gather | bytes 327680 | tf_op jit(solution)/shard_map/pre3/all_gather | solution.py:260
  145.6 3.4 %all-to-all-start.4 = ((f32[4,8,512]{2,1,0:T(8,128)}), f32[4,8,512]{2,1,0:T(8,128)S(1)}, u32[]{:S(2)}, u32[]{:S(2)}) async-start(f32[4,8,512]{2,1,0:T(8,128)} %bitcast.44), calls=%async_computation.4 | async-start | bytes 131072 | tf_op jit(solution)/shard_map/g1/all_to_all | solution.py:323
  149.0 3.2 %all-to-all-done.4 = f32[4,8,512]{2,1,0:T(8,128)S(1)} async-done(((f32[4,8,512]{2,1,0:T(8,128)}), f32[4,8,512]{2,1,0:T(8,128)S(1)}, u32[]{:S(2)}, u32[]{:S(2)}) %all-to-all-start.4) | async-done | bytes 65568 | tf_op jit(solution)/shard_map/g1/all_to_all | solution.py:323
  153.2 9.3 %all-to-all-start.5 = ((bf16[64,32,128]{2,1,0:T(8,128)(2,1)}), bf16[64,32,128]{2,1,0:T(8,128)(2,1)S(1)}, u32[]{:S(2)}, u32[]{:S(2)}) async-start(bf16[64,32,128]{2,1,0:T(8,128)(2,1)} %broadcast_in_dim.129), calls=%async_computation.5 | async-start | bytes 1048576 | tf_op jit(solution)/shard_map/g1/all_to_all | solution.py:53
  165.6 15.6 %all-to-all-done.5 = bf16[64,32,128]{2,1,0:T(8,128)(2,1)S(1)} async-done(((bf16[64,32,128]{2,1,0:T(8,128)(2,1)}), bf16[64,32,128]{2,1,0:T(8,128)(2,1)S(1)}, u32[]{:S(2)}, u32[]{:S(2)}) %all-to-all-start.5) | async-done | bytes 524320 | tf_op jit(solution)/shard_map/g1/all_to_all | solution.py:53
  181.2 6.3 %all-to-all-start.3 = ((bf16[64,48,128]{2,1,0:T(8,128)(2,1)}), bf16[64,48,128]{2,1,0:T(8,128)(2,1)S(1)}, u32[]{:S(2)}, u32[]{:S(2)}) async-start(bf16[64,48,128]{2,1,0:T(8,128)(2,1)} %maximum_maximum_fusion), calls=%async_computation.3 | async-start | bytes 1572864 | tf_op jit(solution)/shard_map/regroup/all_to_all | solution.py:53
  188.3 17.8 %all_gather.25 = f32[72,2048]{1,0:T(8,128)S(1)} all-gather(f32[72,512]{1,0:T(8,128)S(1)} %fusion.29), channel_id=1, replica_groups=mesh['scen'=4,'tile'=64] {'scen'}, dimensions={1}, use_global_device_ids=true | all-gather | bytes 737280 | tf_op jit(solution)/shard_map/weight_grads/all_gather | solution.py:342
  207.5 1.7 all-to-all-done.3
  210.3 9.7 %all-gather.2 = f32[160,640]{1,0:T(8,128)S(1)} all-gather(f32[40,640]{1,0:T(8,128)S(1)} %pad_maximum_fusion), channel_id=4, replica_groups=mesh['scen'=4,'tile'=64] {'scen'}, dimensions={0}, use_global_device_ids=true | all-gather | bytes 512000 | tf_op jit(solution)/shard_map/weight_grads/all_gather | solution.py:337
  (234 shorter events, 57.8 us)
Async XLA Ops:
  2.1 37.3 %collective-permute-start.17 = (f32[5,512]{1,0:T(8,128)S(1)}, f32[5,512]{1,0:T(8,128)S(1)}, u32[]{:S(2)}, u32[]{:S(2)}) collective-permute-start(f32[5,512]{1,0:T(8,128)S(1)} %pad_maximum_fusion.4), channel_id=1, source_target_pairs={{1,0},{2,1},{3,2},{4,3},{5,4},{6,5},{7,6},{8,7},{9,8},{10,9},{11,1... | collective-permute-start | bytes 30728 | tf_op jit(solution)/shard_map/operator/ppermute | solution.py:202
  3.4 42.4 %collective-permute-start.16 = (f32[5,512]{1,0:T(8,128)S(1)}, f32[5,512]{1,0:T(8,128)S(1)}, u32[]{:S(2)}, u32[]{:S(2)}) collective-permute-start(f32[5,512]{1,0:T(8,128)S(1)} %pad_maximum_fusion.4), channel_id=1, source_target_pairs={{0,1},{1,2},{2,3},{3,4},{4,5},{5,6},{6,7},{7,8},{8,9},{9,10},{10,1... | collective-permute-start | bytes 30728 | tf_op jit(solution)/shard_map/operator/ppermute | solution.py:201
  8.8 48.2 %collective-permute-start = (bf16[1,32,512]{2,1,0:T(8,128)(2,1)S(1)}, bf16[1,32,512]{2,1,0:T(8,128)(2,1)S(1)}, u32[]{:S(2)}, u32[]{:S(2)}) collective-permute-start(bf16[1,32,512]{2,1,0:T(8,128)(2,1)S(1)} %dynamic-slice_bitcast_fusion), channel_id=1, source_target_pairs={{16,0},{17,1},{18,2},{19,3},{20,4},{21,5},{22,6},{23,7},{24,8},{25... | collective-permute-start | bytes 98312 | tf_op jit(solution)/shard_map/weights/ppermute | solution.py:34
  19.4 37.7 %collective-permute-start.1 = (bf16[1,32,512]{2,1,0:T(8,128)(2,1)S(1)}, bf16[1,32,512]{2,1,0:T(8,128)(2,1)S(1)}, u32[]{:S(2)}, u32[]{:S(2)}) collective-permute-start(bf16[1,32,512]{2,1,0:T(8,128)(2,1)S(1)} %dynamic-slice_bitcast_fusion), channel_id=1, source_target_pairs={{32,0},{33,1},{34,2},{35,3},{36,4},{37,5},{38,6},{39,7},{40,8},{41... | collective-permute-start | bytes 98312 | tf_op jit(solution)/shard_map/weights/ppermute | solution.py:34
  19.4 37.7 %collective-permute-start.2 = (bf16[1,32,512]{2,1,0:T(8,128)(2,1)S(1)}, bf16[1,32,512]{2,1,0:T(8,128)(2,1)S(1)}, u32[]{:S(2)}, u32[]{:S(2)}) collective-permute-start(bf16[1,32,512]{2,1,0:T(8,128)(2,1)S(1)} %dynamic-slice_bitcast_fusion), channel_id=1, source_target_pairs={{48,0},{49,1},{50,2},{51,3},{52,4},{53,5},{54,6},{55,7},{56,8},{57... | collective-permute-start | bytes 98312 | tf_op jit(solution)/shard_map/weights/ppermute | solution.py:34
  23.7 49.7 %all-to-all-start = ((f32[64,8,128]{2,1,0:T(8,128)}), f32[64,8,128]{2,1,0:T(8,128)S(1)}, u32[]{:S(2)}, u32[]{:S(2)}) async-start(f32[64,8,128]{2,1,0:T(8,128)} %broadcast_in_dim.109), calls=%async_computation | async-start | bytes 524288 | tf_op jit(solution)/shard_map/biases/all_to_all | solution.py:53
  39.4 21.3 %collective-permute-start.9 = (bf16[32,512]{1,0:T(8,128)(2,1)S(1)}, bf16[32,512]{1,0:T(8,128)(2,1)S(1)}, u32[]{:S(2)}, u32[]{:S(2)}) collective-permute-start(bf16[32,512]{1,0:T(8,128)(2,1)S(1)} %copy-done.18), channel_id=1, source_target_pairs={{0,0},{1,1},{2,2},{3,3},{4,4},{5,5},{6,6},{7,7},{8,8},{9,9},{10,10... | collective-permute-start | bytes 98312 | tf_op jit(solution)/shard_map/weights/ppermute | solution.py:192
  57.1 27.9 %collective-permute-start.3 = (bf16[4,1,32,512]{3,2,1,0:T(8,128)(2,1)S(1)}, bf16[4,1,32,512]{3,2,1,0:T(8,128)(2,1)S(1)}, u32[]{:S(2)}, u32[]{:S(2)}) collective-permute-start(bf16[4,1,32,512]{3,2,1,0:T(8,128)(2,1)S(1)} %bitcast_dynamic-update-slice_fusion), channel_id=1, source_target_pairs={{1,0},{2,1},{3,2},{0,3},{5,4},{6,5},{7,6},{4,7},{9,8},{10,9},{11,1... | collective-permute-start | bytes 393224 | tf_op jit(solution)/shard_map/weights/ppermute | solution.py:34
  59.6 26.6 %collective-permute-start.4 = (bf16[4,1,32,512]{3,2,1,0:T(8,128)(2,1)S(1)}, bf16[4,1,32,512]{3,2,1,0:T(8,128)(2,1)S(1)}, u32[]{:S(2)}, u32[]{:S(2)}) collective-permute-start(bf16[4,1,32,512]{3,2,1,0:T(8,128)(2,1)S(1)} %bitcast_dynamic-update-slice_fusion), channel_id=1, source_target_pairs={{2,0},{3,1},{0,2},{1,3},{6,4},{7,5},{4,6},{5,7},{10,8},{11,9},{8,1... | collective-permute-start | bytes 393224 | tf_op jit(solution)/shard_map/weights/ppermute | solution.py:34
  60.1 26.0 %collective-permute-start.5 = (bf16[4,1,32,512]{3,2,1,0:T(8,128)(2,1)S(1)}, bf16[4,1,32,512]{3,2,1,0:T(8,128)(2,1)S(1)}, u32[]{:S(2)}, u32[]{:S(2)}) collective-permute-start(bf16[4,1,32,512]{3,2,1,0:T(8,128)(2,1)S(1)} %bitcast_dynamic-update-slice_fusion), channel_id=1, source_target_pairs={{3,0},{0,1},{1,2},{2,3},{7,4},{4,5},{5,6},{6,7},{11,8},{8,9},{9,10... | collective-permute-start | bytes 393224 | tf_op jit(solution)/shard_map/weights/ppermute | solution.py:34
  60.7 4.6 %collective-permute-start.10 = (bf16[32,512]{1,0:T(8,128)(2,1)S(1)}, bf16[32,512]{1,0:T(8,128)(2,1)S(1)}, u32[]{:S(2)}, u32[]{:S(2)}) collective-permute-start(bf16[32,512]{1,0:T(8,128)(2,1)S(1)} %collective-permute-done.9), channel_id=1, source_target_pairs={{1,0},{2,1},{3,2},{0,3},{5,4},{6,5},{7,6},{4,7},{9,8},{10,9},{11,1... | collective-permute-start | bytes 98312 | tf_op jit(solution)/shard_map/weights/ppermute | solution.py:34
  62.8 4.5 %collective-permute-start.11 = (bf16[32,512]{1,0:T(8,128)(2,1)S(1)}, bf16[32,512]{1,0:T(8,128)(2,1)S(1)}, u32[]{:S(2)}, u32[]{:S(2)}) collective-permute-start(bf16[32,512]{1,0:T(8,128)(2,1)S(1)} %collective-permute-done.9), channel_id=1, source_target_pairs={{2,0},{3,1},{0,2},{1,3},{6,4},{7,5},{4,6},{5,7},{10,8},{11,9},{8,1... | collective-permute-start | bytes 98312 | tf_op jit(solution)/shard_map/weights/ppermute | solution.py:34
  65.4 4.4 %collective-permute-start.12 = (bf16[32,512]{1,0:T(8,128)(2,1)S(1)}, bf16[32,512]{1,0:T(8,128)(2,1)S(1)}, u32[]{:S(2)}, u32[]{:S(2)}) collective-permute-start(bf16[32,512]{1,0:T(8,128)(2,1)S(1)} %collective-permute-done.9), channel_id=1, source_target_pairs={{3,0},{0,1},{1,2},{2,3},{7,4},{4,5},{5,6},{6,7},{11,8},{8,9},{9,10... | collective-permute-start | bytes 98312 | tf_op jit(solution)/shard_map/weights/ppermute | solution.py:34
  70.4 18.8 %collective-permute-start.13 = (bf16[128,512]{1,0:T(8,128)(2,1)}, bf16[128,512]{1,0:T(8,128)(2,1)}, u32[]{:S(2)}, u32[]{:S(2)}) collective-permute-start(bf16[128,512]{1,0:T(8,128)(2,1)} %constant_dynamic-update-slice_fusion.4), channel_id=1, source_target_pairs={{4,0},{5,1},{6,2},{7,3},{8,4},{9,5},{10,6},{11,7},{12,8},{13,9},{1... | collective-permute-start | bytes 393224 | tf_op jit(solution)/shard_map/weights/ppermute | solution.py:34
  72.9 18.8 %collective-permute-start.14 = (bf16[128,512]{1,0:T(8,128)(2,1)}, bf16[128,512]{1,0:T(8,128)(2,1)}, u32[]{:S(2)}, u32[]{:S(2)}) collective-permute-start(bf16[128,512]{1,0:T(8,128)(2,1)} %constant_dynamic-update-slice_fusion.4), channel_id=1, source_target_pairs={{8,0},{9,1},{10,2},{11,3},{12,4},{13,5},{14,6},{15,7},{0,8},{1,9},... | collective-permute-start | bytes 393224 | tf_op jit(solution)/shard_map/weights/ppermute | solution.py:34
  73.4 25.5 %all-to-all-start.1 = ((bf16[64,32,128]{2,1,0:T(8,128)(2,1)}), bf16[64,32,128]{2,1,0:T(8,128)(2,1)S(1)}, u32[]{:S(2)}, u32[]{:S(2)}) async-start(bf16[64,32,128]{2,1,0:T(8,128)(2,1)} %reshape.360), calls=%async_computation.1 | async-start | bytes 1048576 | tf_op jit(solution)/shard_map/first_layer/all_to_all | solution.py:53
  85.1 7.6 %collective-permute-start.15 = (bf16[128,512]{1,0:T(8,128)(2,1)}, bf16[128,512]{1,0:T(8,128)(2,1)S(1)}, u32[]{:S(2)}, u32[]{:S(2)}) collective-permute-start(bf16[128,512]{1,0:T(8,128)(2,1)} %constant_dynamic-update-slice_fusion.4), channel_id=1, source_target_pairs={{12,0},{13,1},{14,2},{15,3},{0,4},{1,5},{2,6},{3,7},{4,8},{5,9},{6... | collective-permute-start | bytes 393224 | tf_op jit(solution)/shard_map/weights/ppermute | solution.py:34
  86.2 37.1 %collective-permute-start.8 = (bf16[512,512]{1,0:T(8,128)(2,1)S(1)}, bf16[512,512]{1,0:T(8,128)(2,1)S(1)}, u32[]{:S(2)}, u32[]{:S(2)}) collective-permute-start(bf16[512,512]{1,0:T(8,128)(2,1)S(1)} %bitcast.154), channel_id=1, source_target_pairs={{12,0},{13,1},{14,2},{15,3},{0,4},{1,5},{2,6},{3,7},{4,8},{5,9},{6... | collective-permute-start | bytes 1572872 | tf_op jit(solution)/shard_map/weights/ppermute | solution.py:34
  87.5 36.0 %collective-permute-start.7 = (bf16[512,512]{1,0:T(8,128)(2,1)S(1)}, bf16[512,512]{1,0:T(8,128)(2,1)S(1)}, u32[]{:S(2)}, u32[]{:S(2)}) collective-permute-start(bf16[512,512]{1,0:T(8,128)(2,1)S(1)} %bitcast.155), channel_id=1, source_target_pairs={{8,0},{9,1},{10,2},{11,3},{12,4},{13,5},{14,6},{15,7},{0,8},{1,9},... | collective-permute-start | bytes 1572872 | tf_op jit(solution)/shard_map/weights/ppermute | solution.py:34
  89.2 34.5 %collective-permute-start.6 = (bf16[512,512]{1,0:T(8,128)(2,1)S(1)}, bf16[512,512]{1,0:T(8,128)(2,1)S(1)}, u32[]{:S(2)}, u32[]{:S(2)}) collective-permute-start(bf16[512,512]{1,0:T(8,128)(2,1)S(1)} %bitcast.156), channel_id=1, source_target_pairs={{4,0},{5,1},{6,2},{7,3},{8,4},{9,5},{10,6},{11,7},{12,8},{13,9},{1... | collective-permute-start | bytes 1572872 | tf_op jit(solution)/shard_map/weights/ppermute | solution.py:34
  99.8 27.1 %all-to-all-start.2 = ((f32[64,16,128]{2,1,0:T(8,128)}), f32[64,16,128]{2,1,0:T(8,128)S(1)}, u32[]{:S(2)}, u32[]{:S(2)}) async-start(f32[64,16,128]{2,1,0:T(8,128)} %maximum_maximum_fusion.1), calls=%async_computation.2 | async-start | bytes 1048576 | tf_op jit(solution)/shard_map/operator/all_to_all | solution.py:53
  145.6 6.7 %all-to-all-start.4 = ((f32[4,8,512]{2,1,0:T(8,128)}), f32[4,8,512]{2,1,0:T(8,128)S(1)}, u32[]{:S(2)}, u32[]{:S(2)}) async-start(f32[4,8,512]{2,1,0:T(8,128)} %bitcast.44), calls=%async_computation.4 | async-start | bytes 131072 | tf_op jit(solution)/shard_map/g1/all_to_all | solution.py:323
  153.2 28.0 %all-to-all-start.5 = ((bf16[64,32,128]{2,1,0:T(8,128)(2,1)}), bf16[64,32,128]{2,1,0:T(8,128)(2,1)S(1)}, u32[]{:S(2)}, u32[]{:S(2)}) async-start(bf16[64,32,128]{2,1,0:T(8,128)(2,1)} %broadcast_in_dim.129), calls=%async_computation.5 | async-start | bytes 1048576 | tf_op jit(solution)/shard_map/g1/all_to_all | solution.py:53
  181.2 28.0 %all-to-all-start.3 = ((bf16[64,48,128]{2,1,0:T(8,128)(2,1)}), bf16[64,48,128]{2,1,0:T(8,128)(2,1)S(1)}, u32[]{:S(2)}, u32[]{:S(2)}) async-start(bf16[64,48,128]{2,1,0:T(8,128)(2,1)} %maximum_maximum_fusion), calls=%async_computation.3 | async-start | bytes 1572864 | tf_op jit(solution)/shard_map/regroup/all_to_all | solution.py:53
  (21 other events, 240.8 us)
